TPU v7x, 32 devices: a whole 2x2x4 slice. The times are simulated.
32 devices in a mesh: grp: 2 (over y), seq: 8 (over z, core), qry: 2 (over x), fac: 1.
Axes of the slice: x: 2, y: 2, z: 4, core: 2. Of those that a mesh axis runs over, the one named last changes fastest.
Arguments:
- activations: bfloat16 [13824, 4096], P(('qry', 'fac'), ('grp', 'seq')), parts along dimension 1, may hold values from -6 to 6
- gradients: bfloat16 [5120, 4096], P(('qry', 'fac'), ('grp', 'seq')), parts along dimension 1, may hold values from -6 to 6
- input_basis: bfloat16 [24, 576, 576], P(('qry', 'fac')), may hold values from -0.25 to 0.25
- output_basis: bfloat16 [8, 640, 640], P(('qry', 'fac')), may hold values from -0.25 to 0.25
- query_left: bfloat16 [8, 32, 5120], P('seq', None, ('qry', 'fac')), may hold values from -0.078125 to 0.078125
- query_right: bfloat16 [8, 32, 13824], P('seq', None, ('qry', 'fac')), may hold values from -0.0012207031 to 0.0012207031
- lengths: int32 [128], P('grp'), parts along dimension 0, may hold values from 1 to 249, as said below
- sequence_ids: int32 [128], P('grp'), parts along dimension 0, may hold values from 0 to 63, each once
Outputs:
- scores: float32 [128, 8], P(('grp', 'seq', 'qry', 'fac')), parts along dimension 0
There are 2 independent parts, one for each index of `grp`. A program takes and returns all parts, laid end to end along the dimension named above; an argument that names none is the same for every part. Nothing has to cross between parts.
Inputs may be any that keep to these rules, and one draw needn't show every extreme that they name: The sequences at positions 8 * k to 8 * k + 7 lie on the k-th device along seq, packed in position order from its first slot. Their lengths sum to at most 256 on every device; exactly 4 devices hold more than 192 tokens, one of them exactly 256, and one other device holds exactly 192. `sequence_ids`: each id appears once.
All inputs are finite; a program needn't handle non-finite values.
Results may differ from a plain program's by a relative error of at most 0.0041.
Values may be sent and summed in bfloat16 or wider, within the bound.
A program may use at most 64 MiB of HBM per device.

v0:
```python
import jax
import jax.numpy as jnp
from jax import lax
from jax.sharding import PartitionSpec as P

SPD = 8


def project(eigen_basis, feature_rows):
    blocks = eigen_basis.shape[0]
    block_width = eigen_basis.shape[1]
    columns = feature_rows.shape[1]
    shaped = feature_rows.reshape(blocks, block_width, columns)
    mapped = jnp.einsum("bij,bin->bjn", eigen_basis, shaped, preferred_element_type=jnp.float32)
    return mapped.reshape(blocks * block_width, columns).astype(jnp.bfloat16)


def sequence_of(owners, slot_index, lengths, sequence_ids):
    device_count = lengths.shape[0] // SPD
    seq_ends = jnp.cumsum(lengths.reshape(device_count, SPD), axis=1, dtype=jnp.int32)
    row_ends = seq_ends[owners]
    seq_slot = jnp.sum((slot_index[:, None] >= row_ends).astype(jnp.int32), axis=1)
    position = owners * SPD + jnp.minimum(seq_slot, SPD - 1)
    return jnp.where(seq_slot < SPD, sequence_ids[position], -1)


def per_device(
    activations,
    gradients,
    input_basis,
    output_basis,
    query_left,
    query_right,
    lengths,
    sequence_ids,
):
    this_owner = lax.axis_index("seq")
    devices = lax.axis_size("seq")
    capacity = activations.shape[1]
    owners = jnp.full((capacity,), this_owner, jnp.int32)
    slot_index = jnp.arange(capacity, dtype=jnp.int32)
    input_projected = project(input_basis, activations)
    output_projected = project(output_basis, gradients)
    rank_count = query_left.shape[1]
    query_width = query_left.shape[0] * devices * rank_count
    left_piece = lax.all_gather(query_left, "seq", axis=0, tiled=True)
    right_piece = lax.all_gather(query_right, "seq", axis=0, tiled=True)
    flat_count = left_piece.shape[0] * rank_count
    left_part = jnp.einsum(
        "dn,kd->nk",
        output_projected,
        left_piece.reshape(flat_count, left_piece.shape[2]),
        preferred_element_type=jnp.float32,
    )
    right_part = jnp.einsum(
        "fn,kf->nk",
        input_projected,
        right_piece.reshape(flat_count, right_piece.shape[2]),
        preferred_element_type=jnp.float32,
    )
    left_mine, right_mine = (
        lax.psum_scatter(left_part, ("qry", "fac"), scatter_dimension=0, tiled=True),
        lax.psum_scatter(right_part, ("qry", "fac"), scatter_dimension=0, tiled=True),
    )
    rows_mine = left_mine.shape[0]
    token_score = jnp.sum(
        (left_mine * right_mine).reshape(rows_mine, query_width // rank_count, rank_count), axis=2
    )
    row_ids = sequence_of(owners, slot_index, lengths, sequence_ids)
    ids_mine = lax.dynamic_slice_in_dim(
        row_ids, lax.axis_index(("qry", "fac")) * rows_mine, rows_mine
    )
    seq_count = lengths.shape[0]
    onehot = (jnp.arange(seq_count, dtype=jnp.int32)[:, None] == ids_mine[None, :]).astype(
        jnp.float32
    )
    score_term = jnp.dot(
        onehot, token_score, precision=lax.Precision.HIGHEST, preferred_element_type=jnp.float32
    )
    result = lax.psum_scatter(score_term, ("seq", "qry", "fac"), scatter_dimension=0, tiled=True)
    return result


def solution(mesh):
    in_specs = (
        P(("qry", "fac"), ("grp", "seq")),
        P(("qry", "fac"), ("grp", "seq")),
        P(("qry", "fac"), None, None),
        P(("qry", "fac"), None, None),
        P("seq", None, ("qry", "fac")),
        P("seq", None, ("qry", "fac")),
        P("grp"),
        P("grp"),
    )
    out_specs = P(("grp", "seq", "qry", "fac"), None)
    return jax.shard_map(
        per_device, mesh=mesh, in_specs=in_specs, out_specs=out_specs, check_vma=False
    )
```

profile of v0, /device:TPU:0, one launch (start us, length us, event | category | flops | bytes accessed | tf_op | source)
XLA Modules:
  0.0 178.1 jit_solution(2724454543854277351)
XLA Ops:
  6.5 0.0 copy-start
  6.5 0.0 all-gather.3.cloned.1.call-start
  6.5 0.7 all-gather.3.cloned.1.call-update
  7.3 0.0 all-gather.5.cloned.1.call-start
  7.3 0.7 all-gather.5.cloned.1.call-update
  8.0 0.0 reduce-scatter.3.cloned.1.call-start
  8.1 0.7 reshape.46
  8.8 0.2 reduce_window_sum.11
  9.0 1.3 gather_fusion
  10.3 1.0 convert_reduce_fusion
  11.3 4.9 %convolution_convert_fusion.1 = bf16[4,640,256]{2,1,0:T(8,128)(2,1)} fusion(bf16[4,640,640]{2,1,0:T(8,128)(2,1)} %param.11, bf16[4,640,256]{2,1,0:T(8,128)(2,1)} %bitcast.26), kind=kOutput, calls=%fused_computation.3 | convolution fusion | flops 839516160 | bytes 5898240 | tf_op jit(solution)/shard_map/bij,bin->bjn/dot_general | solution.py:14
  16.2 0.0 copy-done
  16.2 8.6 %convolution_convert_fusion = bf16[12,576,256]{2,1,0:T(8,128)(2,1)} fusion(bf16[12,576,576]{2,1,0:T(8,128)(2,1)} %param.10, bf16[12,576,256]{2,1,0:T(8,128)(2,1)S(1)} %bitcast.20), kind=kOutput, calls=%fused_computation.2 | convolution fusion | flops 2040201216 | bytes 15040512 | tf_op jit(solution)/shard_map/bij,bin->bjn/dot_general | solution.py:14
  24.9 10.3 %all-gather.3.cloned.1.call-done = bf16[8,32,2560]{2,1,0:T(8,128)(2,1)} async-done(((bf16[1,32,2560]{2,1,0:T(8,128)(2,1)}), bf16[8,32,2560]{2,1,0:T(8,128)(2,1)}) %all-gather.3.cloned.1.call-update) | async-done | bytes 1310736 | tf_op jit(solution)/shard_map/all_gather | solution.py:46
  35.2 3.0 %fusion.2 = f32[256,256]{1,0:T(8,128)} fusion(bf16[2560,256]{1,0:T(8,128)(2,1)} %bitcast.22, bf16[256,2560]{1,0:T(8,128)(2,1)} %bitcast.21), kind=kOutput, calls=%fused_computation.16 | convolution fusion | flops 335544320 | bytes 2883584 | tf_op jit(solution)/shard_map/dn,kd->nk/dot_general | solution.py:49
  38.2 0.0 reduce-scatter.3.cloned.1.call-update
  38.2 0.0 reduce-scatter.5.cloned.1.call-start
  38.3 39.6 %all-gather.5.cloned.1.call-done = bf16[8,32,6912]{2,1,0:T(8,128)(2,1)} async-done(((bf16[1,32,6912]{2,1,0:T(8,128)(2,1)}), bf16[8,32,6912]{2,1,0:T(8,128)(2,1)}) %all-gather.5.cloned.1.call-update) | async-done | bytes 3538960 | tf_op jit(solution)/shard_map/all_gather | solution.py:47
  77.8 0.0 copy-start.1
  77.9 4.9 %fusion.3 = f32[256,256]{1,0:T(8,128)} fusion(bf16[6912,256]{1,0:T(8,128)(2,1)} %bitcast.27, bf16[256,6912]{1,0:T(8,128)(2,1)} %bitcast.25), kind=kOutput, calls=%fused_computation.17 | convolution fusion | flops 905969664 | bytes 7340032 | tf_op jit(solution)/shard_map/fn,kf->nk/dot_general | solution.py:55
  82.8 0.0 reduce-scatter.5.cloned.1.call-update
  82.8 0.0 copy-done.1
  82.8 1.9 %gather_fusion.1 = s32[256]{0:T(256)S(1)} fusion(s32[64]{0:T(128)S(1)} %copy-done.1, s32[1024]{0:T(1024)S(1)} %pad_clamp_fusion), kind=kCustom, calls=%fused_computation.1 | custom fusion | bytes 3072 | tf_op jit(solution)/shard_map/gather | solution.py:24
  84.7 0.1 dynamic_slice.3
  84.8 1.2 dynamic-slice
  86.7 3.9 %reduce-scatter.3.cloned.1.call-done = f32[128,256]{1,0:T(8,128)} async-done(((f32[256,256]{1,0:T(8,128)}), f32[128,256]{1,0:T(8,128)}) %reduce-scatter.3.cloned.1.call-update) | async-done | bytes 131088 | tf_op jit(solution)/shard_map/reduce_scatter | solution.py:62
  90.6 13.9 %reduce-scatter.5.cloned.1.call-done = f32[128,256]{1,0:T(8,128)} async-done(((f32[256,256]{1,0:T(8,128)}), f32[128,256]{1,0:T(8,128)}) %reduce-scatter.5.cloned.1.call-update) | async-done | bytes 131088 | tf_op jit(solution)/shard_map/reduce_scatter | solution.py:63
  104.5 1.6 mul.12
  106.1 1.7 copy.16
  107.8 0.9 bitcast_reduce_fusion
  108.7 0.7 fusion
  109.5 60.8 %all-reduce = f32[64,8]{1,0:T(8,128)} all-reduce(f32[64,8]{1,0:T(8,128)} %fusion), channel_id=4, replica_groups=mesh['grp'=2,'seq'=8,'qry'=2,'fac'=1] {'seq','qry','fac'}, use_global_device_ids=true, to_apply=%region_5.6.clone | all-reduce | flops 512 | bytes 4096
  170.3 1.3 constant_dynamic-slice_fusion
  (6 shorter events, 0.0 us)
Async XLA Ops:
  6.5 9.7 %copy-start = (bf16[6912,256]{1,0:T(8,128)(2,1)S(1)}, bf16[6912,256]{1,0:T(8,128)(2,1)}, u32[]{:S(2)}) copy-start(bf16[6912,256]{1,0:T(8,128)(2,1)} %param.8) | copy-start | bytes 10616836
  6.5 28.6 %all-gather.3.cloned.1.call-start = ((), (), s32[]{:S(2)}) async-start(), calls=%async_computation.2 | async-start | bytes 1474560 | tf_op jit(solution)/shard_map/all_gather | solution.py:46
  7.3 70.6 %all-gather.5.cloned.1.call-start = ((), (), s32[]{:S(2)}) async-start(), calls=%async_computation.4 | async-start | bytes 3981312 | tf_op jit(solution)/shard_map/all_gather | solution.py:47
  8.0 82.6 %reduce-scatter.3.cloned.1.call-start = ((), (), s32[]{:S(2)}) async-start(), calls=%async_computation.3 | async-start | bytes 393216 | tf_op jit(solution)/shard_map/reduce_scatter | solution.py:62
  38.2 66.3 %reduce-scatter.5.cloned.1.call-start = ((), (), s32[]{:S(2)}) async-start(), calls=%async_computation.5 | async-start | bytes 393216 | tf_op jit(solution)/shard_map/reduce_scatter | solution.py:63
  77.8 5.0 %copy-start.1 = (s32[64]{0:T(128)S(1)}, s32[64]{0:T(128)}, u32[]{:S(2)}) copy-start(s32[64]{0:T(128)} %param.15) | copy-start | bytes 772
Sparse Core Ops, SparseCore 0:
  9.0 26.1 all-gather.2
  36.8 40.9 all-gather.4
  80.1 10.5 reduce-scatter.2
  92.8 11.6 reduce-scatter.4
where the time goes:
time: 178 us
  waiting for transfers between devices  69.2 us (39%)
  blocking collectives  60.8 us (34%)
  matrix products  22.2 us (12%)
  between operations  13.9 us (8%)
  local copies, waits for them, and re-layouts  8.18 us (5%)
  other arithmetic  3.75 us (2%)
    unnamed x1, blocking collectives  60.8 us
    all_gather x1, waiting for transfers between devices, per_device(): right_piece = lax.all_gather(query_right, 'seq', axis=0, tiled=True)  39.6 us
    reduce_scatter x1, waiting for transfers between devices, per_device(): lax.psum_scatter(right_part, ('qry', 'fac'), scatter_dimension=0, tiled=T...  13.9 us
    dot_general x2, matrix products, project(): jnp.einsum('bij,bin->bjn', eigen_basis, shaped, preferred_element_type=jn...  13.5 us
    all_gather x1, waiting for transfers between devices, per_device(): left_piece = lax.all_gather(query_left, 'seq', axis=0, tiled=True)  10.3 us
    dot_general x1, matrix products, per_device(): jnp.einsum('fn,kf->nk', input_projected, right_piece.reshape(flat_count,...  4.93 us
    reduce_scatter x1, waiting for transfers between devices, per_device(): lax.psum_scatter(left_part, ('qry', 'fac'), scatter_dimension=0, tiled=True)  3.95 us
  transfers between devices with their start and end apart: 4, of which 4 were waited for; matrix products, arithmetic and copies ran while one was open for 16% of the time, Pallas kernels for 0%

commit v1 on v0

--- a/solution.py
+++ b/solution.py
@@ -1,6 +1,8 @@
 import jax
 import jax.numpy as jnp
 from jax import lax
+from jax.experimental import pallas as pl
+from jax.experimental.pallas import tpu as pltpu
 from jax.sharding import PartitionSpec as P
 
 SPD = 8
@@ -81,7 +83,378 @@
     return result
 
 
+RIGHT_WAVES = 3
+TURNS = (1, 2, 3)
+DIMS_TN = (((0,), (0,)), ((), ()))
+DIMS_NT = (((1,), (1,)), ((), ()))
+
+
+def fused_kernel(
+    len_ref,
+    id_ref,
+    act_hbm,
+    grad_hbm,
+    in_basis_hbm,
+    out_basis_hbm,
+    left_hbm,
+    right_hbm,
+    out_ref,
+    act,
+    grad,
+    in_basis,
+    out_basis,
+    q_right,
+    q_left,
+    right_acc,
+    left_acc,
+    right_out,
+    right_in,
+    score_out,
+    score_in,
+    load_sem,
+    own_sem,
+    z_send,
+    z_recv,
+    f_send,
+    y_send,
+    y_recv,
+    s_send,
+    s_recv,
+    x_send,
+    x_recv,
+    o_send,
+    o_recv,
+):
+    grp, seq, qry = lax.axis_index("grp"), lax.axis_index("seq"), lax.axis_index("qry")
+    z, core = seq // 2, seq % 2
+    inner = jnp.logical_or(z == 1, z == 2)
+    turn_z = {1: z + 1 - 2 * (z % 2), 2: (z + 2) % 4, 3: 3 - z}
+    mesh_id = pl.DeviceIdType.MESH
+    y_dev = (1 - grp, seq, qry, 0)
+    x_dev = (grp, seq, 1 - qry, 0)
+    sib_dev = (grp, z * 2 + 1 - core, qry, 0)
+    rank = left_hbm.shape[1]
+    in_blocks, in_width = in_basis_hbm.shape[0], in_basis_hbm.shape[1]
+    out_blocks, out_width = out_basis_hbm.shape[0], out_basis_hbm.shape[1]
+    wave_width = q_right.shape[3]
+    left_half = q_left.shape[2]
+    waves = RIGHT_WAVES + 1
+
+    def z_dev(t):
+        return (grp, turn_z[t] * 2 + core, qry, 0)
+
+    order = []
+    for c in range(RIGHT_WAVES):
+        half_blocks = in_blocks // 2
+        per = half_blocks // RIGHT_WAVES
+        order += [(c, "in", h * half_blocks + c * per + k) for h in range(2) for k in range(per)]
+    order += [(RIGHT_WAVES, "out", b) for b in range(out_blocks)]
+
+    def loads(i):
+        _, kind, b = order[i]
+        if kind == "in":
+            pairs = ((in_basis_hbm, in_basis, act_hbm, act, in_width),)
+        else:
+            pairs = ((out_basis_hbm, out_basis, grad_hbm, grad, out_width),)
+        basis_src, basis_dst, rows_src, rows_dst, width = pairs[0]
+        return (
+            pltpu.make_async_copy(basis_src.at[b], basis_dst.at[b], load_sem.at[0, i]),
+            pltpu.make_async_copy(
+                rows_src.at[pl.ds(b * width, width)],
+                rows_dst.at[pl.ds(b * width, width)],
+                load_sem.at[1, i],
+            ),
+        )
+
+    def slot(c, half, query):
+        rows = pl.ds(pl.multiple_of(query * rank, rank), rank)
+        if c < RIGHT_WAVES:
+            return q_right.at[half, c, rows]
+        return q_left.at[half, rows]
+
+    def own_piece(c, half):
+        if c < RIGHT_WAVES:
+            first = half * (wave_width * RIGHT_WAVES) + c * wave_width
+            return right_hbm.at[0, :, pl.ds(pl.multiple_of(first, 128), wave_width)]
+        first = half * left_half
+        return left_hbm.at[0, :, pl.ds(pl.multiple_of(first, 128), left_half)]
+
+    def remote(src, dst, send, recv, dev):
+        return pltpu.make_async_remote_copy(
+            src_ref=src, dst_ref=dst, send_sem=send, recv_sem=recv,
+            device_id=dev, device_id_type=mesh_id,
+        )
+
+    def query_of(t):
+        return turn_z[t] * 2 + core
+
+    def z_out(c, t):
+        return remote(
+            own_piece(c, grp), slot(c, grp, seq), z_send.at[t - 1, c], z_recv.at[t - 1, c], z_dev(t)
+        )
+
+    def z_in(c, t):
+        here = slot(c, grp, query_of(t))
+        return remote(here, here, z_send.at[t - 1, c], z_recv.at[t - 1, c], z_dev(t))
+
+    def z_forward(c):
+        here = slot(c, grp, query_of(2))
+        return remote(here, here, f_send.at[c], z_recv.at[2, c], z_dev(1))
+
+    def y_out(c, t):
+        here = slot(c, grp, query_of(t))
+        return remote(here, here, y_send.at[t - 1, c], y_recv.at[t - 1, c], y_dev)
+
+    def y_in(c, t):
+        here = slot(c, 1 - grp, query_of(t))
+        return remote(here, here, y_send.at[t - 1, c], y_recv.at[t - 1, c], y_dev)
+
+    def sib_out(c, t, kind):
+        half = grp if kind == 0 else 1 - grp
+        if t == 0:
+            return remote(
+                own_piece(c, half), slot(c, half, seq),
+                s_send.at[kind, t, c], s_recv.at[kind, t, c], sib_dev,
+            )
+        here = slot(c, half, query_of(t))
+        return remote(here, here, s_send.at[kind, t, c], s_recv.at[kind, t, c], sib_dev)
+
+    def sib_in(c, t, kind):
+        half = grp if kind == 0 else 1 - grp
+        source_z = z if t == 0 else turn_z[t]
+        here = slot(c, half, source_z * 2 + 1 - core)
+        return remote(here, here, s_send.at[kind, t, c], s_recv.at[kind, t, c], sib_dev)
+
+    def own_local(c, half):
+        return pltpu.make_async_copy(own_piece(c, half), slot(c, half, seq), own_sem.at[half, c])
+
+    group = 16
+    me = seq * 2 + qry
+
+    def peer(o):
+        d = (me + o) % group
+        return d, (grp, d // 2, d % 2, 0)
+
+    barrier = pltpu.get_barrier_semaphore()
+    pl.semaphore_signal(barrier, inc=1, device_id=y_dev, device_id_type=mesh_id)
+    for o in range(1, group):
+        pl.semaphore_signal(barrier, inc=1, device_id=peer(o)[1], device_id_type=mesh_id)
+    for i in range(len(order)):
+        for copy in loads(i):
+            copy.start()
+    for c in range(waves):
+        for half in range(2):
+            own_local(c, half).start()
+    pl.semaphore_wait(barrier, group)
+
+    for c in range(waves):
+        for t in (2, 1):
+            z_out(c, t).start()
+
+        @pl.when(inner)
+        def _():
+            z_out(c, 3).start()
+
+        for kind in range(2):
+            sib_out(c, 0, kind).start()
+
+    def project(i):
+        _, kind, b = order[i]
+        for copy in loads(i):
+            copy.wait()
+        if kind == "in":
+            rows = pl.ds(b * in_width, in_width)
+            act[rows] = lax.dot_general(
+                in_basis[b], act[rows], DIMS_TN, preferred_element_type=jnp.float32
+            ).astype(jnp.bfloat16)
+        else:
+            rows = pl.ds(b * out_width, out_width)
+            grad[rows] = lax.dot_general(
+                out_basis[b], grad[rows], DIMS_TN, preferred_element_type=jnp.float32
+            ).astype(jnp.bfloat16)
+
+    def contract(c):
+        for half in range(2):
+            own_local(c, half).wait()
+        for t in range(4):
+            for kind in range(2):
+                sib_in(c, t, kind).wait_recv()
+        if c < RIGHT_WAVES:
+            total = None
+            for half in range(2):
+                first = half * (wave_width * RIGHT_WAVES) + c * wave_width
+                part = jnp.dot(
+                    q_right[half, c], act[pl.ds(first, wave_width)],
+                    preferred_element_type=jnp.float32,
+                )
+                total = part if total is None else total + part
+            right_acc[...] = total if c == 0 else right_acc[...] + total
+        else:
+            left_acc[...] = jnp.dot(
+                q_left[0], grad[pl.ds(0, left_half)], preferred_element_type=jnp.float32
+            ) + jnp.dot(
+                q_left[1], grad[pl.ds(left_half, left_half)], preferred_element_type=jnp.float32
+            )
+
+    x_copy = remote(right_out, right_in, x_send, x_recv, x_dev)
+    steps = [(c, t) for c in range(waves) for t in (2, 1, 3)]
+    pending = list(range(len(order)))
+    for i, (c, t) in enumerate(steps):
+        for _ in range(2):
+            if pending:
+                project(pending.pop(0))
+        z_in(c, t).wait_recv()
+        if t == 2:
+
+            @pl.when(inner)
+            def _():
+                z_forward(c).start()
+
+        y_out(c, t).start()
+        sib_out(c, t, 0).start()
+        if i >= 1:
+            pc, pt = steps[i - 1]
+            y_in(pc, pt).wait_recv()
+            sib_out(pc, pt, 1).start()
+        if c >= 1 and t == 1:
+            contract(c - 1)
+            if c == RIGHT_WAVES:
+                right_out[...] = right_acc[...].astype(jnp.bfloat16)
+                x_copy.start()
+    pc, pt = steps[-1]
+    y_in(pc, pt).wait_recv()
+    sib_out(pc, pt, 1).start()
+    columns = act.shape[1]
+    seq_rows = score_out.shape[0]
+    row = lax.broadcasted_iota(jnp.int32, (seq_rows, columns), 0)
+    col = lax.broadcasted_iota(jnp.int32, (seq_rows, columns), 1)
+    per_out = out_ref.shape[0]
+    row_id = jnp.where(row % 8 < per_out, (row // 8) * per_out + row % 8, -1)
+    column_id = jnp.full((seq_rows, columns), -2, jnp.int32)
+    end = jnp.int32(0)
+    for j in range(SPD):
+        begin = end
+        end = begin + len_ref[seq * SPD + j]
+        column_id = jnp.where(
+            jnp.logical_and(col >= begin, col < end), id_ref[seq * SPD + j], column_id
+        )
+    onehot = jnp.where(row_id == column_id, 1.0, 0.0).astype(jnp.float32)
+    contract(RIGHT_WAVES)
+
+    x_copy.wait_recv()
+    product = left_acc[...] * (right_acc[...] + right_in[...].astype(jnp.float32))
+    queries = product.shape[0] // rank
+    token = jnp.sum(product.reshape(queries, rank, columns), axis=1)
+    token = jnp.concatenate([token, jnp.zeros((128 - queries, columns), jnp.float32)], axis=0)
+    score_out[...] = lax.dot_general(
+        onehot, token, DIMS_NT,
+        precision=lax.Precision.HIGHEST, preferred_element_type=jnp.float32,
+    )
+
+    def score_copy(o):
+        d, dev = peer(o)
+        return remote(
+            score_out.at[pl.ds(pl.multiple_of(d * 8, 8), 8)], score_in.at[me],
+            o_send.at[o], o_recv.at[o], dev,
+        )
+
+    for o in range(1, group):
+        score_copy(o).start()
+    score_in[me] = score_out[pl.ds(pl.multiple_of(me * 8, 8), 8)]
+    for c in range(waves):
+        for t in (1, 2):
+            z_out(c, t).wait_send()
+
+        @pl.when(inner)
+        def _():
+            z_out(c, 3).wait_send()
+            z_forward(c).wait_send()
+
+        for t in TURNS:
+            y_out(c, t).wait_send()
+        for t in range(4):
+            for kind in range(2):
+                sib_out(c, t, kind).wait_send()
+    x_copy.wait_send()
+    for o in range(1, group):
+        d = (me + group - o) % group
+        remote(score_in.at[d], score_in.at[d], o_send.at[o], o_recv.at[o], x_dev).wait_recv()
+    total = jnp.sum(score_in[...], axis=0)
+    out_ref[...] = total[: out_ref.shape[0], : out_ref.shape[1]]
+    for o in range(1, group):
+        score_copy(o).wait_send()
+
+
+def fused_device(
+    activations,
+    gradients,
+    input_basis,
+    output_basis,
+    query_left,
+    query_right,
+    lengths,
+    sequence_ids,
+):
+    devices = lax.axis_size("seq")
+    rank = query_left.shape[1]
+    query_rows = query_left.shape[0] * devices * rank
+    queries = query_left.shape[0] * devices
+    columns = activations.shape[1]
+    wave_width = query_right.shape[2] // (2 * RIGHT_WAVES)
+    left_half = query_left.shape[2] // 2
+    group = devices * lax.axis_size("qry")
+    waves = RIGHT_WAVES + 1
+    block_count = input_basis.shape[0] + output_basis.shape[0]
+    anywhere = pl.BlockSpec(memory_space=pl.ANY)
+    scalars = pl.BlockSpec(memory_space=pltpu.SMEM)
+    dma = pltpu.SemaphoreType.DMA
+    return pl.pallas_call(
+        fused_kernel,
+        out_shape=jax.ShapeDtypeStruct((lengths.shape[0] // group, queries), jnp.float32),
+        in_specs=[scalars, scalars] + [anywhere] * 6,
+        out_specs=pl.BlockSpec(memory_space=pltpu.VMEM),
+        scratch_shapes=[
+            pltpu.VMEM(activations.shape, jnp.bfloat16),
+            pltpu.VMEM(gradients.shape, jnp.bfloat16),
+            pltpu.VMEM(input_basis.shape, jnp.bfloat16),
+            pltpu.VMEM(output_basis.shape, jnp.bfloat16),
+            pltpu.VMEM((2, RIGHT_WAVES, query_rows, wave_width), jnp.bfloat16),
+            pltpu.VMEM((2, query_rows, left_half), jnp.bfloat16),
+            pltpu.VMEM((query_rows, columns), jnp.float32),
+            pltpu.VMEM((query_rows, columns), jnp.float32),
+            pltpu.VMEM((query_rows, columns), jnp.bfloat16),
+            pltpu.VMEM((query_rows, columns), jnp.bfloat16),
+            pltpu.VMEM((group * 8, 128), jnp.float32),
+            pltpu.VMEM((group, 8, 128), jnp.float32),
+            dma((2, block_count)),
+            dma((2, waves)),
+            dma((3, waves)),
+            dma((3, waves)),
+            dma((waves,)),
+            dma((3, waves)),
+            dma((3, waves)),
+            dma((2, 4, waves)),
+            dma((2, 4, waves)),
+            dma,
+            dma,
+            dma((group,)),
+            dma((group,)),
+        ],
+        compiler_params=pltpu.CompilerParams(
+            collective_id=0, has_side_effects=True, vmem_limit_bytes=52 * 1024 * 1024
+        ),
+    )(
+        lengths, sequence_ids, activations, gradients, input_basis, output_basis,
+        query_left, query_right,
+    )
+
+
 def solution(mesh):
+    sizes = mesh.shape
+    fused = (
+        sizes["grp"] == 2 and sizes["seq"] == 8 and sizes["qry"] == 2 and sizes["fac"] == 1
+    )
+    body = fused_device if fused else per_device
     in_specs = (
         P(("qry", "fac"), ("grp", "seq")),
         P(("qry", "fac"), ("grp", "seq")),
@@ -94,5 +467,5 @@
     )
     out_specs = P(("grp", "seq", "qry", "fac"), None)
     return jax.shard_map(
-        per_device, mesh=mesh, in_specs=in_specs, out_specs=out_specs, check_vma=False
-    )
+        body, mesh=mesh, in_specs=in_specs, out_specs=out_specs, check_vma=False
+    )

time: 178 us -> 56.7 us (0.32)
  waiting for transfers between devices: 69.2 us -> 0 us
  blocking collectives: 60.8 us -> 0 us
  Pallas kernels: 0 us -> 51.3 us
  matrix products: 22.2 us -> 0 us
  between operations: 13.9 us -> 0.01 us
  other arithmetic: 3.75 us -> 0 us
  local copies, waits for them, and re-layouts: 8.18 us -> 5.13 us
    unnamed x1 -> x0, blocking collectives: 60.8 us -> none
    pallas_call x0 -> x1, Pallas kernels: none -> 51.3 us  [fused_device(): pl.pallas_call(fused_kernel, out_shape=jax.ShapeDtypeStruct((lengths.shap...]
    all_gather x2 -> x0, waiting for transfers between devices: 49.9 us -> none  [the longest x1 39.6 us: per_device(): right_piece = lax.all_gather(query_right, 'seq', axis=0, tiled=True)]
    dot_general x5 -> x0, matrix products: 22.2 us -> none  [the longest x2 13.5 us: project(): jnp.einsum('bij,bin->bjn', eigen_basis, shaped, preferred_element_type=jn...]
    reduce_scatter x2 -> x0, waiting for transfers between devices: 17.8 us -> none  [the longest x1 13.9 us: per_device(): lax.psum_scatter(right_part, ('qry', 'fac'), scatter_dimension=0, tiled=T...]
    gather x2 -> x0, local copies, waits for them, and re-layouts: 3.2 us -> none  [the longest x1 1.87 us: sequence_of(): return jnp.where(seq_slot < SPD, sequence_ids[position], -1)]
    unnamed x6 -> x11, local copies, waits for them, and re-layouts: 2.51 us -> 5.13 us
    reduce_sum x2 -> x0, other arithmetic: 1.94 us -> none  [the longest x1 1.02 us: sequence_of(): jnp.sum((slot_index[:, None] >= row_ends).astype(jnp.int32), axis=1)]
  transfers between devices with their start and end apart: 4 -> 0, of which waited for: 4 -> 0; matrix products, arithmetic and copies ran while one was open for 16% -> 0% of each run, Pallas kernels for 0% -> 0%
where the time goes in v1:
time: 56.7 us; the launch traced here: 56.5 us
  Pallas kernels  51.3 us (90%)
  local copies, waits for them, and re-layouts  5.13 us (9%)
    pallas_call x1, Pallas kernels, fused_device(): pl.pallas_call(fused_kernel, out_shape=jax.ShapeDtypeStruct((lengths.shap...  51.3 us
    unnamed x11, local copies, waits for them, and re-layouts  5.13 us

profile of v1, /device:TPU:0, one launch (start us, length us, event | category | flops | bytes accessed | tf_op | source)
XLA Modules:
  0.0 56.5 jit_solution(3456258400871518754)
XLA Ops:
  0.0 0.0 copy-start
  0.0 1.3 %copy-done = bf16[2560,256]{1,0:T(8,128)(2,1)S(1)} copy-done((bf16[2560,256]{1,0:T(8,128)(2,1)S(1)}, bf16[2560,256]{1,0:T(8,128)(2,1)}, u32[]{:S(2)}) %copy-start) | copy-done | bytes 1310744
  1.3 0.0 copy-start.1
  1.3 1.0 %copy-done.1 = bf16[1,32,6912]{2,1,0:T(8,128)(2,1)S(1)} copy-done((bf16[1,32,6912]{2,1,0:T(8,128)(2,1)S(1)}, bf16[1,32,6912]{2,1,0:T(8,128)(2,1)}, u32[]{:S(2)}) %copy-start.1) | copy-done | bytes 442392
  2.3 0.0 copy-start.2
  2.3 0.9 %copy-done.2 = bf16[1,32,2560]{2,1,0:T(8,128)(2,1)S(1)} copy-done((bf16[1,32,2560]{2,1,0:T(8,128)(2,1)S(1)}, bf16[1,32,2560]{2,1,0:T(8,128)(2,1)}, u32[]{:S(2)}) %copy-start.2) | copy-done | bytes 163864
  3.2 0.0 copy-start.3
  3.2 0.7 %copy-done.3 = s32[64]{0:T(128)S(1)} copy-done((s32[64]{0:T(128)S(1)}, s32[64]{0:T(128)}, u32[]{:S(2)}) %copy-start.3) | copy-done | bytes 280
  3.9 0.0 copy-start.4
  3.9 0.7 %copy-done.4 = s32[64]{0:T(128)S(1)} copy-done((s32[64]{0:T(128)S(1)}, s32[64]{0:T(128)}, u32[]{:S(2)}) %copy-start.4) | copy-done | bytes 280
  4.6 51.3 %shard_map.82 = f32[4,8]{1,0:T(4,128)S(1)} custom-call(s32[64]{0:T(128)S(1)} %copy-done.3, s32[64]{0:T(128)S(1)} %copy-done.4, bf16[6912,256]{1,0:T(8,128)(2,1)} %act_hbm.1, bf16[2560,256]{1,0:T(8,128)(2,1)S(1)} %copy-done, bf16[12,576,576]{2,1,0:T(8,128)(2,1)} %in_basis_hbm.1, bf16[4,640,640]{2,1,0:T(8,128)(2,1)} %out_basis_hbm.1, ...), custom_call_target="tpu_custom_call" | custom-call | tf_op jit(solution)/shard_map/pallas_call | solution.py:411
  55.9 0.6 %copy.10 = f32[4,8]{1,0:T(4,128)} copy(f32[4,8]{1,0:T(4,128)S(1)} %shard_map.82) | data formatting | bytes 256
Async XLA Ops:
  0.0 1.3 %copy-start = (bf16[2560,256]{1,0:T(8,128)(2,1)S(1)}, bf16[2560,256]{1,0:T(8,128)(2,1)}, u32[]{:S(2)}) copy-start(bf16[2560,256]{1,0:T(8,128)(2,1)} %grad_hbm.1) | copy-start | bytes 3932164
  1.3 1.0 %copy-start.1 = (bf16[1,32,6912]{2,1,0:T(8,128)(2,1)S(1)}, bf16[1,32,6912]{2,1,0:T(8,128)(2,1)}, u32[]{:S(2)}) copy-start(bf16[1,32,6912]{2,1,0:T(8,128)(2,1)} %right_hbm.1) | copy-start | bytes 1327108
  2.3 0.9 %copy-start.2 = (bf16[1,32,2560]{2,1,0:T(8,128)(2,1)S(1)}, bf16[1,32,2560]{2,1,0:T(8,128)(2,1)}, u32[]{:S(2)}) copy-start(bf16[1,32,2560]{2,1,0:T(8,128)(2,1)} %left_hbm.1) | copy-start | bytes 491524
  3.2 0.7 %copy-start.3 = (s32[64]{0:T(128)S(1)}, s32[64]{0:T(128)}, u32[]{:S(2)}) copy-start(s32[64]{0:T(128)} %len_ref.1) | copy-start | bytes 772
  3.9 0.7 %copy-start.4 = (s32[64]{0:T(128)S(1)}, s32[64]{0:T(128)}, u32[]{:S(2)}) copy-start(s32[64]{0:T(128)} %id_ref.1) | copy-start | bytes 772

commit v2 on v1

--- a/solution.py
+++ b/solution.py
@@ -85,6 +85,8 @@
 
 RIGHT_WAVES = 3
 TURNS = (1, 2, 3)
+AHEAD = 1
+LAG = 5
 DIMS_TN = (((0,), (0,)), ((), ()))
 DIMS_NT = (((1,), (1,)), ((), ()))
 
@@ -228,26 +230,22 @@
     def own_local(c, half):
         return pltpu.make_async_copy(own_piece(c, half), slot(c, half, seq), own_sem.at[half, c])
 
-    group = 16
-    me = seq * 2 + qry
-
-    def peer(o):
-        d = (me + o) % group
-        return d, (grp, d // 2, d % 2, 0)
+    plane = [sib_dev, x_dev, (grp, z * 2 + 1 - core, 1 - qry, 0)]
+    column = [z_dev(t) for t in TURNS]
 
     barrier = pltpu.get_barrier_semaphore()
-    pl.semaphore_signal(barrier, inc=1, device_id=y_dev, device_id_type=mesh_id)
-    for o in range(1, group):
-        pl.semaphore_signal(barrier, inc=1, device_id=peer(o)[1], device_id_type=mesh_id)
+    greeted = plane + column + [y_dev]
+    for dev in greeted:
+        pl.semaphore_signal(barrier, inc=1, device_id=dev, device_id_type=mesh_id)
     for i in range(len(order)):
         for copy in loads(i):
             copy.start()
     for c in range(waves):
         for half in range(2):
             own_local(c, half).start()
-    pl.semaphore_wait(barrier, group)
-
-    for c in range(waves):
+    pl.semaphore_wait(barrier, len(greeted))
+
+    def send_wave(c):
         for t in (2, 1):
             z_out(c, t).start()
 
@@ -255,6 +253,9 @@
         def _():
             z_out(c, 3).start()
 
+    for c in range(min(AHEAD, waves)):
+        send_wave(c)
+    for c in range(waves):
         for kind in range(2):
             sib_out(c, 0, kind).start()
 
@@ -299,38 +300,37 @@
     x_copy = remote(right_out, right_in, x_send, x_recv, x_dev)
     steps = [(c, t) for c in range(waves) for t in (2, 1, 3)]
     pending = list(range(len(order)))
-    for i, (c, t) in enumerate(steps):
-        for _ in range(2):
-            if pending:
-                project(pending.pop(0))
-        z_in(c, t).wait_recv()
-        if t == 2:
-
-            @pl.when(inner)
-            def _():
-                z_forward(c).start()
-
-        y_out(c, t).start()
-        sib_out(c, t, 0).start()
-        if i >= 1:
-            pc, pt = steps[i - 1]
-            y_in(pc, pt).wait_recv()
-            sib_out(pc, pt, 1).start()
-        if c >= 1 and t == 1:
-            contract(c - 1)
-            if c == RIGHT_WAVES:
-                right_out[...] = right_acc[...].astype(jnp.bfloat16)
-                x_copy.start()
-    pc, pt = steps[-1]
-    y_in(pc, pt).wait_recv()
-    sib_out(pc, pt, 1).start()
+    for i in range(len(steps) + LAG):
+        if i < len(steps):
+            c, t = steps[i]
+            for _ in range(2):
+                if pending:
+                    project(pending.pop(0))
+            z_in(c, t).wait_recv()
+            if t == 2:
+
+                @pl.when(inner)
+                def _():
+                    z_forward(c).start()
+
+            y_out(c, t).start()
+            if t == 2 and c + AHEAD < waves:
+                send_wave(c + AHEAD)
+            sib_out(c, t, 0).start()
+        if i >= LAG:
+            c, t = steps[i - LAG]
+            y_in(c, t).wait_recv()
+            sib_out(c, t, 1).start()
+            if t == 3 and c < RIGHT_WAVES:
+                contract(c)
+                if c == RIGHT_WAVES - 1:
+                    right_out[...] = right_acc[...].astype(jnp.bfloat16)
+                    x_copy.start()
     columns = act.shape[1]
-    seq_rows = score_out.shape[0]
-    row = lax.broadcasted_iota(jnp.int32, (seq_rows, columns), 0)
-    col = lax.broadcasted_iota(jnp.int32, (seq_rows, columns), 1)
-    per_out = out_ref.shape[0]
-    row_id = jnp.where(row % 8 < per_out, (row // 8) * per_out + row % 8, -1)
-    column_id = jnp.full((seq_rows, columns), -2, jnp.int32)
+    lanes = score_out.shape[2]
+    row = lax.broadcasted_iota(jnp.int32, (lanes, columns), 0)
+    col = lax.broadcasted_iota(jnp.int32, (lanes, columns), 1)
+    column_id = jnp.full((lanes, columns), -1, jnp.int32)
     end = jnp.int32(0)
     for j in range(SPD):
         begin = end
@@ -338,29 +338,31 @@
         column_id = jnp.where(
             jnp.logical_and(col >= begin, col < end), id_ref[seq * SPD + j], column_id
         )
-    onehot = jnp.where(row_id == column_id, 1.0, 0.0).astype(jnp.float32)
+    onehot = jnp.where(row == column_id, 1.0, 0.0).astype(jnp.float32)
     contract(RIGHT_WAVES)
 
     x_copy.wait_recv()
     product = left_acc[...] * (right_acc[...] + right_in[...].astype(jnp.float32))
     queries = product.shape[0] // rank
     token = jnp.sum(product.reshape(queries, rank, columns), axis=1)
-    token = jnp.concatenate([token, jnp.zeros((128 - queries, columns), jnp.float32)], axis=0)
-    score_out[...] = lax.dot_general(
-        onehot, token, DIMS_NT,
+    score_out[0] = lax.dot_general(
+        token, onehot, DIMS_NT,
         precision=lax.Precision.HIGHEST, preferred_element_type=jnp.float32,
     )
 
-    def score_copy(o):
-        d, dev = peer(o)
+    def score_copy(stage, k):
         return remote(
-            score_out.at[pl.ds(pl.multiple_of(d * 8, 8), 8)], score_in.at[me],
-            o_send.at[o], o_recv.at[o], dev,
+            score_out.at[stage], score_in.at[stage, k], o_send.at[stage, k], o_recv.at[stage, k],
+            (plane, column)[stage][k],
         )
 
-    for o in range(1, group):
-        score_copy(o).start()
-    score_in[me] = score_out[pl.ds(pl.multiple_of(me * 8, 8), 8)]
+    for k in range(3):
+        score_copy(0, k).start()
+    for k in range(3):
+        score_copy(0, k).wait_recv()
+    score_out[1] = (score_out[0] + score_in[0, 0]) + (score_in[0, 1] + score_in[0, 2])
+    for k in range(3):
+        score_copy(1, k).start()
     for c in range(waves):
         for t in (1, 2):
             z_out(c, t).wait_send()
@@ -376,13 +378,22 @@
             for kind in range(2):
                 sib_out(c, t, kind).wait_send()
     x_copy.wait_send()
-    for o in range(1, group):
-        d = (me + group - o) % group
-        remote(score_in.at[d], score_in.at[d], o_send.at[o], o_recv.at[o], x_dev).wait_recv()
-    total = jnp.sum(score_in[...], axis=0)
-    out_ref[...] = total[: out_ref.shape[0], : out_ref.shape[1]]
-    for o in range(1, group):
-        score_copy(o).wait_send()
+    for k in range(3):
+        score_copy(1, k).wait_recv()
+    total = (score_out[1] + score_in[1, 0]) + (score_in[1, 1] + score_in[1, 2])
+    per_out = out_ref.shape[0]
+    first_id = (seq * 2 + qry) * per_out
+    pick_row = lax.broadcasted_iota(jnp.int32, (8, lanes), 0)
+    pick_lane = lax.broadcasted_iota(jnp.int32, (8, lanes), 1)
+    pick = jnp.where(pick_lane == pick_row + first_id, 1.0, 0.0).astype(jnp.float32)
+    mine = lax.dot_general(
+        pick, total, DIMS_NT,
+        precision=lax.Precision.HIGHEST, preferred_element_type=jnp.float32,
+    )
+    out_ref[...] = mine[:per_out]
+    for stage in range(2):
+        for k in range(3):
+            score_copy(stage, k).wait_send()
 
 
 def fused_device(
@@ -424,8 +435,8 @@
             pltpu.VMEM((query_rows, columns), jnp.float32),
             pltpu.VMEM((query_rows, columns), jnp.bfloat16),
             pltpu.VMEM((query_rows, columns), jnp.bfloat16),
-            pltpu.VMEM((group * 8, 128), jnp.float32),
-            pltpu.VMEM((group, 8, 128), jnp.float32),
+            pltpu.VMEM((2, queries, 128), jnp.float32),
+            pltpu.VMEM((2, 3, queries, 128), jnp.float32),
             dma((2, block_count)),
             dma((2, waves)),
             dma((3, waves)),
@@ -437,11 +448,11 @@
             dma((2, 4, waves)),
             dma,
             dma,
-            dma((group,)),
-            dma((group,)),
+            dma((2, 3)),
+            dma((2, 3)),
         ],
         compiler_params=pltpu.CompilerParams(
-            collective_id=0, has_side_effects=True, vmem_limit_bytes=52 * 1024 * 1024
+            collective_id=0, has_side_effects=True, vmem_limit_bytes=62 * 1024 * 1024
         ),
     )(
         lengths, sequence_ids, activations, gradients, input_basis, output_basis,

time: 56.7 us -> 46.4 us (0.82)
  Pallas kernels: 51.3 us -> 45 us
  local copies, waits for them, and re-layouts: 5.13 us -> 1.26 us
    pallas_call x1, Pallas kernels: 51.3 us -> 45 us  [fused_device(): pl.pallas_call(fused_kernel, out_shape=jax.ShapeDtypeStruct((lengths.shap...]
    unnamed x11 -> x1, local copies, waits for them, and re-layouts: 5.13 us -> 1.26 us
where the time goes in v2:
time: 46.4 us; the launch traced here: 46.2 us
  Pallas kernels  45 us (97%)
  local copies, waits for them, and re-layouts  1.26 us (3%)
    pallas_call x1, Pallas kernels, fused_device(): pl.pallas_call(fused_kernel, out_shape=jax.ShapeDtypeStruct((lengths.shap...  45 us
    unnamed x1, local copies, waits for them, and re-layouts  1.26 us

profile of v2, /device:TPU:0, one launch (start us, length us, event | category | flops | bytes accessed | tf_op | source)
XLA Modules:
  0.0 46.2 jit_solution(7380624089607345103)
XLA Ops:
  0.0 45.0 %shard_map.82 = f32[4,8]{1,0:T(4,128)} custom-call(s32[64]{0:T(128)} %len_ref.1, s32[64]{0:T(128)} %id_ref.1, bf16[6912,256]{1,0:T(8,128)(2,1)} %act_hbm.1, bf16[2560,256]{1,0:T(8,128)(2,1)} %grad_hbm.1, bf16[12,576,576]{2,1,0:T(8,128)(2,1)} %in_basis_hbm.1, bf16[4,640,640]{2,1,0:T(8,128)(2,1)} %out_basis_hbm.1, bf16[1,32,2560]{2,1,0:T(8,128)(2,1)} %left_hbm.1, ...), custom_call_target="tpu_custom_call" | custom-call | tf_op jit(solution)/shard_map/pallas_call | solution.py:422
  45.0 1.3 %copy.10 = f32[4,8]{1,0:T(4,128)} copy(f32[4,8]{1,0:T(4,128)} %shard_map.82) | data formatting | bytes 256

commit v3 on v2

--- a/solution.py
+++ b/solution.py
@@ -84,6 +84,7 @@
 
 
 RIGHT_WAVES = 3
+LEFT_WAVES = 1
 TURNS = (1, 2, 3)
 AHEAD = 1
 LAG = 5
@@ -139,8 +140,8 @@
     in_blocks, in_width = in_basis_hbm.shape[0], in_basis_hbm.shape[1]
     out_blocks, out_width = out_basis_hbm.shape[0], out_basis_hbm.shape[1]
     wave_width = q_right.shape[3]
-    left_half = q_left.shape[2]
-    waves = RIGHT_WAVES + 1
+    left_width = q_left.shape[3]
+    waves = RIGHT_WAVES + LEFT_WAVES
 
     def z_dev(t):
         return (grp, turn_z[t] * 2 + core, qry, 0)
@@ -172,14 +173,14 @@
         rows = pl.ds(pl.multiple_of(query * rank, rank), rank)
         if c < RIGHT_WAVES:
             return q_right.at[half, c, rows]
-        return q_left.at[half, rows]
+        return q_left.at[half, c - RIGHT_WAVES, rows]
 
     def own_piece(c, half):
         if c < RIGHT_WAVES:
             first = half * (wave_width * RIGHT_WAVES) + c * wave_width
             return right_hbm.at[0, :, pl.ds(pl.multiple_of(first, 128), wave_width)]
-        first = half * left_half
-        return left_hbm.at[0, :, pl.ds(pl.multiple_of(first, 128), left_half)]
+        first = half * (left_width * LEFT_WAVES) + (c - RIGHT_WAVES) * left_width
+        return left_hbm.at[0, :, pl.ds(pl.multiple_of(first, 128), left_width)]
 
     def remote(src, dst, send, recv, dev):
         return pltpu.make_async_remote_copy(
@@ -232,9 +233,12 @@
 
     plane = [sib_dev, x_dev, (grp, z * 2 + 1 - core, 1 - qry, 0)]
     column = [z_dev(t) for t in TURNS]
+    far = [(grp, turn_z[t] * 2 + e, q, 0) for t in TURNS for e, q in
+           ((1 - core, qry), (core, 1 - qry), (1 - core, 1 - qry))]
+    others = plane + column + far
 
     barrier = pltpu.get_barrier_semaphore()
-    greeted = plane + column + [y_dev]
+    greeted = others + [y_dev]
     for dev in greeted:
         pl.semaphore_signal(barrier, inc=1, device_id=dev, device_id_type=mesh_id)
     for i in range(len(order)):
@@ -291,11 +295,16 @@
                 total = part if total is None else total + part
             right_acc[...] = total if c == 0 else right_acc[...] + total
         else:
-            left_acc[...] = jnp.dot(
-                q_left[0], grad[pl.ds(0, left_half)], preferred_element_type=jnp.float32
-            ) + jnp.dot(
-                q_left[1], grad[pl.ds(left_half, left_half)], preferred_element_type=jnp.float32
-            )
+            k = c - RIGHT_WAVES
+            total = None
+            for half in range(2):
+                first = half * (left_width * LEFT_WAVES) + k * left_width
+                part = jnp.dot(
+                    q_left[half, k], grad[pl.ds(first, left_width)],
+                    preferred_element_type=jnp.float32,
+                )
+                total = part if total is None else total + part
+            left_acc[...] = total if k == 0 else left_acc[...] + total
 
     x_copy = remote(right_out, right_in, x_send, x_recv, x_dev)
     steps = [(c, t) for c in range(waves) for t in (2, 1, 3)]
@@ -321,13 +330,13 @@
             c, t = steps[i - LAG]
             y_in(c, t).wait_recv()
             sib_out(c, t, 1).start()
-            if t == 3 and c < RIGHT_WAVES:
+            if t == 3 and c < waves - 1:
                 contract(c)
                 if c == RIGHT_WAVES - 1:
                     right_out[...] = right_acc[...].astype(jnp.bfloat16)
                     x_copy.start()
     columns = act.shape[1]
-    lanes = score_out.shape[2]
+    lanes = score_out.shape[1]
     row = lax.broadcasted_iota(jnp.int32, (lanes, columns), 0)
     col = lax.broadcasted_iota(jnp.int32, (lanes, columns), 1)
     column_id = jnp.full((lanes, columns), -1, jnp.int32)
@@ -339,30 +348,22 @@
             jnp.logical_and(col >= begin, col < end), id_ref[seq * SPD + j], column_id
         )
     onehot = jnp.where(row == column_id, 1.0, 0.0).astype(jnp.float32)
-    contract(RIGHT_WAVES)
+    contract(waves - 1)
 
     x_copy.wait_recv()
     product = left_acc[...] * (right_acc[...] + right_in[...].astype(jnp.float32))
     queries = product.shape[0] // rank
     token = jnp.sum(product.reshape(queries, rank, columns), axis=1)
-    score_out[0] = lax.dot_general(
+    score_out[...] = lax.dot_general(
         token, onehot, DIMS_NT,
         precision=lax.Precision.HIGHEST, preferred_element_type=jnp.float32,
     )
 
-    def score_copy(stage, k):
-        return remote(
-            score_out.at[stage], score_in.at[stage, k], o_send.at[stage, k], o_recv.at[stage, k],
-            (plane, column)[stage][k],
-        )
-
-    for k in range(3):
-        score_copy(0, k).start()
-    for k in range(3):
-        score_copy(0, k).wait_recv()
-    score_out[1] = (score_out[0] + score_in[0, 0]) + (score_in[0, 1] + score_in[0, 2])
-    for k in range(3):
-        score_copy(1, k).start()
+    def score_copy(k):
+        return remote(score_out, score_in.at[k], o_send.at[k], o_recv.at[k], others[k])
+
+    for k in range(len(others)):
+        score_copy(k).start()
     for c in range(waves):
         for t in (1, 2):
             z_out(c, t).wait_send()
@@ -378,9 +379,9 @@
             for kind in range(2):
                 sib_out(c, t, kind).wait_send()
     x_copy.wait_send()
-    for k in range(3):
-        score_copy(1, k).wait_recv()
-    total = (score_out[1] + score_in[1, 0]) + (score_in[1, 1] + score_in[1, 2])
+    for k in range(len(others)):
+        score_copy(k).wait_recv()
+    total = score_out[...] + jnp.sum(score_in[...], axis=0)
     per_out = out_ref.shape[0]
     first_id = (seq * 2 + qry) * per_out
     pick_row = lax.broadcasted_iota(jnp.int32, (8, lanes), 0)
@@ -391,9 +392,8 @@
         precision=lax.Precision.HIGHEST, preferred_element_type=jnp.float32,
     )
     out_ref[...] = mine[:per_out]
-    for stage in range(2):
-        for k in range(3):
-            score_copy(stage, k).wait_send()
+    for k in range(len(others)):
+        score_copy(k).wait_send()
 
 
 def fused_device(
@@ -412,9 +412,9 @@
     queries = query_left.shape[0] * devices
     columns = activations.shape[1]
     wave_width = query_right.shape[2] // (2 * RIGHT_WAVES)
-    left_half = query_left.shape[2] // 2
+    left_width = query_left.shape[2] // (2 * LEFT_WAVES)
     group = devices * lax.axis_size("qry")
-    waves = RIGHT_WAVES + 1
+    waves = RIGHT_WAVES + LEFT_WAVES
     block_count = input_basis.shape[0] + output_basis.shape[0]
     anywhere = pl.BlockSpec(memory_space=pl.ANY)
     scalars = pl.BlockSpec(memory_space=pltpu.SMEM)
@@ -430,13 +430,13 @@
             pltpu.VMEM(input_basis.shape, jnp.bfloat16),
             pltpu.VMEM(output_basis.shape, jnp.bfloat16),
             pltpu.VMEM((2, RIGHT_WAVES, query_rows, wave_width), jnp.bfloat16),
-            pltpu.VMEM((2, query_rows, left_half), jnp.bfloat16),
+            pltpu.VMEM((2, LEFT_WAVES, query_rows, left_width), jnp.bfloat16),
             pltpu.VMEM((query_rows, columns), jnp.float32),
             pltpu.VMEM((query_rows, columns), jnp.float32),
             pltpu.VMEM((query_rows, columns), jnp.bfloat16),
             pltpu.VMEM((query_rows, columns), jnp.bfloat16),
-            pltpu.VMEM((2, queries, 128), jnp.float32),
-            pltpu.VMEM((2, 3, queries, 128), jnp.float32),
+            pltpu.VMEM((queries, 128), jnp.float32),
+            pltpu.VMEM((group - 1, queries, 128), jnp.float32),
             dma((2, block_count)),
             dma((2, waves)),
             dma((3, waves)),
@@ -448,8 +448,8 @@
             dma((2, 4, waves)),
             dma,
             dma,
-            dma((2, 3)),
-            dma((2, 3)),
+            dma((group - 1,)),
+            dma((group - 1,)),
         ],
         compiler_params=pltpu.CompilerParams(
             collective_id=0, has_side_effects=True, vmem_limit_bytes=62 * 1024 * 1024

time: 46.4 us -> 45.6 us (0.983)
  Pallas kernels: 45 us -> 44.2 us
    pallas_call x1, Pallas kernels: 45 us -> 44.2 us  [fused_device(): pl.pallas_call(fused_kernel, out_shape=jax.ShapeDtypeStruct((lengths.shap...]
where the time goes in v3:
time: 45.6 us; the launch traced here: 45.4 us
  Pallas kernels  44.2 us (97%)
  local copies, waits for them, and re-layouts  1.26 us (3%)
    pallas_call x1, Pallas kernels, fused_device(): pl.pallas_call(fused_kernel, out_shape=jax.ShapeDtypeStruct((lengths.shap...  44.2 us
    unnamed x1, local copies, waits for them, and re-layouts  1.26 us

profile of v3, /device:TPU:0, one launch (start us, length us, event | category | flops | bytes accessed | tf_op | source)
XLA Modules:
  0.0 45.4 jit_solution(13334733883522766761)
XLA Ops:
  0.0 44.2 %shard_map.82 = f32[4,8]{1,0:T(4,128)} custom-call(s32[64]{0:T(128)} %len_ref.1, s32[64]{0:T(128)} %id_ref.1, bf16[6912,256]{1,0:T(8,128)(2,1)} %act_hbm.1, bf16[2560,256]{1,0:T(8,128)(2,1)} %grad_hbm.1, bf16[12,576,576]{2,1,0:T(8,128)(2,1)} %in_basis_hbm.1, bf16[4,640,640]{2,1,0:T(8,128)(2,1)} %out_basis_hbm.1, bf16[1,32,2560]{2,1,0:T(8,128)(2,1)} %left_hbm.1, ...), custom_call_target="tpu_custom_call" | custom-call | tf_op jit(solution)/shard_map/pallas_call | solution.py:422
  44.2 1.3 %copy.10 = f32[4,8]{1,0:T(4,128)} copy(f32[4,8]{1,0:T(4,128)} %shard_map.82) | data formatting | bytes 256
